TPU v7x, 32 devices: a whole 2x2x4 slice. The times are simulated.
32 devices in a mesh: band: 4 (over y, x), pix: 8 (over z, core).
Axes of the slice: x: 2, y: 2, z: 4, core: 2. Of those that a mesh axis runs over, the one named last changes fastest.
Arguments:
- pixels: bfloat16 [128, 8, 1024], P('pix', 'band'), may hold values from -6 to 6
- clear_count: int32 [8], P('pix'), may hold values from 3 to 10, as said below
- clear_index: int32 [80], P('pix'), may hold values from 0 to 15, as said below
- attn_gain: float32 [1024], replicated, may hold values from 0.1 to 1.9
- w_query: bfloat16 [1024, 1024], P(None, 'band')
- w_key: bfloat16 [1024, 1024], P(None, 'band')
- w_value: bfloat16 [1024, 1024], P(None, 'band'), may hold values from -0.1875 to 0.1875
- w_out: bfloat16 [1024, 1024], P('band'), may hold values from -0.1875 to 0.1875
- mlp_gain: float32 [1024], replicated, may hold values from 0.1 to 1.9
- w_gate: bfloat16 [1024, 4096], P(None, 'band'), may hold values from -0.1875 to 0.1875
- w_up: bfloat16 [1024, 4096], P(None, 'band'), may hold values from -0.1875 to 0.1875
- w_down: bfloat16 [4096, 1024], P('band'), may hold values from -0.09375 to 0.09375
Outputs:
- updated: bfloat16 [128, 8, 1024], P('pix', 'band')
Inputs may be any that keep to these rules, and one draw needn't show every extreme that they name: `clear_count`: some tile, drawn from the seed, keeps exactly 10 clear pixels. `clear_index`: for tile t, entries t*10 to t*10+clear_count[t]-1 are distinct local pixel indices in rising order; the tile's remaining entries are 0.
All inputs are finite; a program needn't handle non-finite values.
Results may differ from a plain program's by a relative error of at most 0.019.
Values may be sent and summed in bfloat16 or wider, within the bound.
A program may use at most 64 MiB of HBM per device.

v0:
```python
import jax
import jax.numpy as jnp
from jax import lax
from jax.sharding import PartitionSpec as P

HD = 64


def normed(rows, gain):
    full = rows.astype(jnp.float32)
    scaled = full * lax.rsqrt(jnp.mean(full * full, axis=-1, keepdims=True) + 1e-05)
    return (scaled * gain).astype(jnp.bfloat16)


def slot_live(number, slots_per_tile, counts):
    slot = jnp.arange(number, dtype=jnp.int32)
    owner = slot // slots_per_tile
    owned = owner[:, None] == jnp.arange(counts.shape[0], dtype=jnp.int32)[None, :]
    owner_count = jnp.sum(jnp.where(owned, counts[None, :], 0), axis=1)
    return slot % slots_per_tile < owner_count


def shards(
    pixels,
    clear_count,
    clear_index,
    attn_gain,
    w_query,
    w_key,
    w_value,
    w_out,
    mlp_gain,
    w_gate,
    w_up,
    w_down,
):
    own_count = clear_count[0]
    kept = jnp.take(pixels, clear_index, axis=0)
    kept_rows = jnp.swapaxes(kept, 0, 1)
    all_rows = lax.all_gather(kept_rows, "band", axis=0, tiled=True)
    spec, slots_here, width = all_rows.shape
    heads_here = w_query.shape[1] // HD
    flat = normed(all_rows, attn_gain).reshape(spec * slots_here, width)

    def project(weight):
        out = jnp.dot(flat, weight, preferred_element_type=jnp.float32).astype(jnp.bfloat16)
        return out.reshape(spec, slots_here, heads_here, HD)

    query = project(w_query)
    key = project(w_key)
    value = project(w_value)
    counts = lax.all_gather(clear_count, "pix", axis=0, tiled=True)
    start_top = jnp.full((spec, heads_here, slots_here), -1e30, jnp.float32)
    top = start_top
    key_piece = lax.all_gather(key, "pix", axis=1, tiled=True)
    value_piece = lax.all_gather(value, "pix", axis=1, tiled=True)
    live = slot_live(key_piece.shape[1], slots_here, counts)
    scores = jnp.einsum(
        "sqhd,skhd->shqk", query, key_piece, preferred_element_type=jnp.float32
    ) * HD ** (-0.5)
    masked = jnp.where(live[None, None, None, :], scores, -1e30)
    new_top = jnp.maximum(top, jnp.max(masked, axis=-1))
    expo = jnp.where(live[None, None, None, :], jnp.exp(masked - new_top[..., None]), 0.0)
    totals = jnp.sum(expo, axis=-1)
    mixed = jnp.einsum(
        "shqk,skhd->sqhd",
        expo.astype(jnp.bfloat16),
        value_piece,
        preferred_element_type=jnp.float32,
    )
    acc = mixed
    top, totals, acc = (new_top, totals, acc)
    context = (acc / jnp.transpose(totals, (0, 2, 1))[..., None]).astype(jnp.bfloat16)
    context_rows = context.reshape(spec, slots_here, heads_here * HD)
    spec_here = spec // lax.axis_size("band")
    piece = context_rows
    out = jnp.dot(
        piece.reshape(spec_here * lax.axis_size("band") * slots_here, heads_here * HD),
        w_out,
        preferred_element_type=jnp.float32,
    )
    attn_out = lax.psum_scatter(
        out.reshape(spec_here * lax.axis_size("band"), slots_here, width).astype(jnp.bfloat16),
        "band",
        scatter_dimension=0,
        tiled=True,
    ).astype(jnp.float32)
    state = (kept_rows.astype(jnp.float32) + attn_out).astype(jnp.bfloat16)
    mlp_in = lax.all_gather(normed(state, mlp_gain), "band", axis=0, tiled=True)
    piece = mlp_in.reshape(spec_here * lax.axis_size("band") * slots_here, width)
    gate = jnp.dot(piece, w_gate, preferred_element_type=jnp.float32)
    upper = jnp.dot(piece, w_up, preferred_element_type=jnp.float32)
    hidden = (jax.nn.silu(gate) * upper).astype(jnp.bfloat16)
    out = jnp.dot(hidden, w_down, preferred_element_type=jnp.float32)
    mlp_out = lax.psum_scatter(
        out.reshape(spec_here * lax.axis_size("band"), slots_here, width).astype(jnp.bfloat16),
        "band",
        scatter_dimension=0,
        tiled=True,
    ).astype(jnp.float32)
    encoded = (state.astype(jnp.float32) + mlp_out).astype(jnp.bfloat16)
    live_here = jnp.arange(slots_here, dtype=jnp.int32) < own_count
    chosen = (
        jnp.arange(pixels.shape[0], dtype=jnp.int32)[:, None] == clear_index[None, :]
    ) & live_here[None, :]
    placed = jnp.einsum(
        "pc,scd->psd", chosen.astype(jnp.bfloat16), encoded, preferred_element_type=jnp.float32
    ).astype(jnp.bfloat16)
    taken = jnp.any(chosen, axis=1)
    return jnp.where(taken[:, None, None], placed, pixels)


def solution(mesh):
    return jax.shard_map(
        shards,
        mesh=mesh,
        in_specs=(
            P("pix", "band", None),
            P("pix"),
            P("pix"),
            P(),
            P(None, "band"),
            P(None, "band"),
            P(None, "band"),
            P("band", None),
            P(),
            P(None, "band"),
            P(None, "band"),
            P("band", None),
        ),
        out_specs=P("pix", "band", None),
        check_vma=False,
    )
```

profile of v0, /device:TPU:0, one launch (start us, length us, event | category | flops | bytes accessed | tf_op | source)
XLA Modules:
  0.0 139.1 jit_solution(15242703701285460851)
XLA Ops:
  6.5 0.8 compare_select_fusion
  7.4 0.7 compare_and_fusion
  8.0 1.5 %gather_fusion = bf16[10,2,1024]{2,1,0:T(2,128)(2,1)S(1)} fusion(bf16[16,2,1024]{2,1,0:T(2,128)(2,1)} %param.12, s32[1024]{0:T(1024)S(1)} %pad_clamp_fusion), kind=kCustom, calls=%fused_computation | custom fusion | bytes 81960 | tf_op jit(solution)/shard_map/jit(_take)/gather | solution.py:38
  9.6 10.4 %all_gather.15 = bf16[8,10,1024]{2,1,0:T(8,128)(2,1)S(1)} all-gather(bf16[2,10,1024]{2,1,0:T(8,128)(2,1)S(1)} %fusion.29), channel_id=1, replica_groups=mesh['band'=4,'pix'=8] {'band'}, dimensions={0}, use_global_device_ids=true | all-gather | bytes 204800 | tf_op jit(solution)/shard_map/all_gather | solution.py:40
  20.0 0.1 fusion.7
  20.2 0.8 fusion.9
  21.1 1.3 convolution_convert_fusion.3
  22.4 0.1 reshape.82
  22.5 15.8 %all_gather.18 = bf16[8,80,4,64]{3,0,2,1:T(8,128)(2,1)S(1)} all-gather(bf16[8,10,4,64]{3,0,2,1:T(8,128)(2,1)S(1)} %copy.38), channel_id=1, replica_groups=mesh['band'=4,'pix'=8] {'pix'}, dimensions={1}, use_global_device_ids=true | all-gather | bytes 368640 | tf_op jit(solution)/shard_map/all_gather | solution.py:55
  38.3 0.2 convolution_convert_fusion.4
  39.2 0.7 dynamic-slice
  39.9 0.8 dynamic-update-slice
  40.8 8.7 %all-reduce = s32[8]{0:T(128)S(1)} all-reduce(s32[8]{0:T(128)S(1)} %dynamic-update-slice), channel_id=1, replica_groups=mesh['band'=4,'pix'=8] {'pix'}, use_global_device_ids=true, to_apply=%add | all-reduce | flops 8 | bytes 64
  49.6 0.5 fusion.40
  50.2 1.3 convolution_convert_fusion.5
  51.4 0.1 reshape.80
  51.6 15.2 %all_gather.16 = bf16[8,80,4,64]{3,0,2,1:T(8,128)(2,1)S(1)} all-gather(bf16[8,10,4,64]{3,0,2,1:T(8,128)(2,1)S(1)} %copy.37), channel_id=1, replica_groups=mesh['band'=4,'pix'=8] {'pix'}, dimensions={1}, use_global_device_ids=true | all-gather | bytes 368640 | tf_op jit(solution)/shard_map/all_gather | solution.py:56
  66.8 0.3 fusion.16
  67.1 0.4 fusion.3
  67.6 0.1 reshape.100
  67.7 0.9 convolution_convert_fusion
  68.7 21.8 %reduce-scatter.3.cloned.1.call-done = bf16[2,10,1024]{2,1,0:T(8,128)(2,1)} async-done(((bf16[8,10,1024]{2,1,0:T(8,128)(2,1)}), bf16[2,10,1024]{2,1,0:T(8,128)(2,1)}) %reduce-scatter.3.cloned.1.call-update) | async-done | bytes 40976 | tf_op jit(solution)/shard_map/reduce_scatter | solution.py:82
  90.5 1.0 fusion.19
  91.5 0.9 fusion.21
  92.4 9.3 %all_gather.19 = bf16[8,10,1024]{2,1,0:T(8,128)(2,1)S(1)} all-gather(bf16[2,10,1024]{2,1,0:T(8,128)(2,1)S(1)} %fusion.21), channel_id=1, replica_groups=mesh['band'=4,'pix'=8] {'band'}, dimensions={0}, use_global_device_ids=true | all-gather | bytes 204800 | tf_op jit(solution)/shard_map/all_gather | solution.py:89
  101.8 0.5 fusion.41
  102.3 3.2 %convolution_convert_fusion.1 = bf16[80,1024]{1,0:T(8,128)(2,1)S(1)} fusion(bf16[1024,1024]{1,0:T(8,128)(2,1)} %param.23, bf16[80,1024]{1,0:T(8,128)(2,1)S(1)} %reshape.83, bf16[1024,1024]{1,0:T(8,128)(2,1)} %param.22, f32[80,1024]{1,0:T(8,128)S(1)} %fusion.41), kind=kOutput, calls=%fused_computation.8 | convolution fusion | flops 336117760 | bytes 4849664 | tf_op jit(solution)/shard_map/dot_general | solution.py:94
  105.5 0.8 convert_element_type.74
  106.3 0.1 fusion.32
  106.4 24.1 %reduce-scatter.5.cloned.1.call-done = bf16[2,10,1024]{2,1,0:T(8,128)(2,1)} async-done(((bf16[8,10,1024]{2,1,0:T(8,128)(2,1)}), bf16[2,10,1024]{2,1,0:T(8,128)(2,1)}) %reduce-scatter.5.cloned.1.call-update) | async-done | bytes 40976 | tf_op jit(solution)/shard_map/reduce_scatter | solution.py:95
  130.5 1.1 fusion.4
  131.5 0.7 copy.45
  (36 shorter events, 0.6 us)
Async XLA Ops:
  6.5 95.2 %copy-start = (bf16[1024,1024]{1,0:T(8,128)(2,1)S(1)}, bf16[1024,1024]{1,0:T(8,128)(2,1)}, u32[]{:S(2)}) copy-start(bf16[1024,1024]{1,0:T(8,128)(2,1)} %param.21) | copy-start | bytes 6291460
  6.5 31.8 %copy-start.1 = (bf16[1024,256]{1,0:T(8,128)(2,1)S(1)}, bf16[1024,256]{1,0:T(8,128)(2,1)}, u32[]{:S(2)}) copy-start(bf16[1024,256]{1,0:T(8,128)(2,1)} %param.16) | copy-start | bytes 1572868
  6.5 83.9 %reduce-scatter.3.cloned.1.call-start = ((), (), s32[]{:S(2)}) async-start(), calls=%async_computation.2 | async-start | bytes 327680 | tf_op jit(solution)/shard_map/reduce_scatter | solution.py:82
  9.5 29.7 %copy-start.7 = (u32[32]{0:T(128)S(1)}, u32[32]{0:T(128)}, u32[]{:S(2)}) copy-start(u32[32]{0:T(128)} %constant.63) | copy-start | bytes 388
  51.4 16.3 %copy-start.2 = (bf16[256,1024]{1,0:T(8,128)(2,1)S(1)}, bf16[256,1024]{1,0:T(8,128)(2,1)}, u32[]{:S(2)}) copy-start(bf16[256,1024]{1,0:T(8,128)(2,1)} %param.19) | copy-start | bytes 1572868
  66.8 24.7 %copy-start.5 = (f32[1024]{0:T(1024)S(1)}, f32[1024]{0:T(1024)}, u32[]{:S(2)}) copy-start(f32[1024]{0:T(1024)} %param.20) | copy-start | bytes 12292
  68.7 61.8 %reduce-scatter.5.cloned.1.call-start = ((), (), s32[]{:S(2)}) async-start(), calls=%async_computation.3 | async-start | bytes 327680 | tf_op jit(solution)/shard_map/reduce_scatter | solution.py:95
  102.3 4.0 %copy-start.6 = (s32[10]{0:T(128)S(1)}, s32[10]{0:T(128)}, u32[]{:S(2)}) copy-start(s32[10]{0:T(128)} %param.14) | copy-start | bytes 124
  102.3 28.2 %copy-start.3 = (bf16[2,10,1024]{2,1,0:T(8,128)(2,1)S(1)}, bf16[2,10,1024]{2,1,0:T(8,128)(2,1)}, u32[]{:S(2)}) copy-start(bf16[2,10,1024]{2,1,0:T(8,128)(2,1)} %reduce-scatter.3.cloned.1.call-done) | copy-start | bytes 122884
  102.3 28.2 %copy-start.4 = (bf16[16,2,1024]{2,1,0:T(2,128)(2,1)S(1)}, bf16[16,2,1024]{2,1,0:T(2,128)(2,1)}, u32[]{:S(2)}) copy-start(bf16[16,2,1024]{2,1,0:T(2,128)(2,1)} %param.12) | copy-start | bytes 196612
Sparse Core Ops, SparseCore 0:
  68.8 21.6 reduce-scatter.2
  106.4 24.0 reduce-scatter.4
where the time goes:
time: 140 us; the launch traced here: 139 us
  blocking collectives  59.5 us (42%)
  waiting for transfers between devices  45.9 us (33%)
  between operations  14.3 us (10%)
  matrix products  9.32 us (7%)
  local copies, waits for them, and re-layouts  5.06 us (4%)
  other arithmetic  5 us (4%)
    reduce_scatter x2, waiting for transfers between devices, shards(): lax.psum_scatter(out.reshape(spec_here * lax.axis_size('band'), slots_her...  45.8 us
    all_gather x1, blocking collectives, shards(): key_piece = lax.all_gather(key, 'pix', axis=1, tiled=True)  15.8 us
    all_gather x1, blocking collectives, shards(): value_piece = lax.all_gather(value, 'pix', axis=1, tiled=True)  15.2 us
    all_gather x1, blocking collectives, shards(): all_rows = lax.all_gather(kept_rows, 'band', axis=0, tiled=True)  10.4 us
    all_gather x1, blocking collectives, shards(): mlp_in = lax.all_gather(normed(state, mlp_gain), 'band', axis=0, tiled=True)  9.27 us
    unnamed x1, blocking collectives  8.71 us
    dot_general x1, matrix products, shards(): out = jnp.dot(hidden, w_down, preferred_element_type=jnp.float32)  3.16 us
  transfers between devices with their start and end apart: 2, of which 2 were waited for; matrix products, arithmetic and copies ran while one was open for 0% of the time, Pallas kernels for 0%

commit v1 on v0

v1 whole, which is shorter than its diff:
```python
import functools

import jax
import jax.numpy as jnp
from jax import lax
from jax.experimental import pallas as pl
from jax.experimental.pallas import tpu as pltpu
from jax.sharding import PartitionSpec as P

HD = 64
MESH = pl.DeviceIdType.MESH
BF = jnp.bfloat16
F32 = jnp.float32


def normed(full, gain):
    scaled = full * lax.rsqrt(jnp.mean(full * full, axis=-1, keepdims=True) + 1e-05)
    return (scaled * gain).astype(BF)


def kernel(
    nb, np_, spec_here, tile, caps,
    x_ref, count_ref, index_ref, again_ref, mgain_ref,
    wq_h, wk_h, wv_h, wo_h, wg_h, wu_h, wd_h,
    out_ref,
    wq, wk, wv, wo, wg, wu, wd,
    rows_a, marks, qkv, qkv_in, ctx, ctx_in, part1, part1_in, rows_b, part2, part2_in,
    w_sem,
    ag_s, ag_r, mk_s, mk_r, qk_s, qk_r, cx_s, cx_r, p1_s, p1_r, bg_s, bg_r, p2_s, p2_r,
):
    b, t = lax.axis_index("band"), lax.axis_index("pix")
    mine = spec_here * tile
    width = x_ref.shape[1]
    hq = wq.shape[1]
    heads = hq // HD

    loads = []
    for i, (src, dst) in enumerate(
        ((wq_h, wq), (wk_h, wk), (wv_h, wv), (wo_h, wo), (wg_h, wg), (wu_h, wu), (wd_h, wd))
    ):
        load = pltpu.make_async_copy(src, dst, w_sem.at[i])
        load.start()
        loads.append(load)

    band_peers = [(lax.rem(b + k, nb), t) for k in range(1, nb)]
    pix_peers = [(b, lax.rem(t + k, np_)) for k in range(1, np_)]
    barrier = pltpu.get_barrier_semaphore()
    for peer in band_peers + pix_peers:
        pl.semaphore_signal(barrier, inc=1, device_id=peer, device_id_type=MESH)

    def rows_of(ref, i, n):
        return ref.at[pl.ds(pl.multiple_of(i * n, n), n)]

    my_rows = rows_of(rows_a, b, mine)
    my_rows[...] = normed(x_ref[...].astype(F32), again_ref[...])
    spot = lax.broadcasted_iota(jnp.int32, (tile, 128), 0)
    count = count_ref[0]
    live = jnp.zeros((tile, 128), jnp.int32)
    for c in range(caps):
        live = jnp.where((spot == index_ref[c]) & (c < count), 1, live)
    my_mark = rows_of(marks, t, tile)
    my_mark[...] = live.astype(F32).astype(BF)

    pl.semaphore_wait(barrier, len(band_peers) + len(pix_peers))

    def send(src, dst, s_sem, r_sem, k, peer):
        copy = pltpu.make_async_remote_copy(
            src_ref=src, dst_ref=dst, send_sem=s_sem.at[k], recv_sem=r_sem.at[k],
            device_id=peer, device_id_type=MESH,
        )
        copy.start()
        return copy

    gathers = [send(my_rows, my_rows, ag_s, ag_r, k, p) for k, p in enumerate(band_peers)]
    mark_sends = [send(my_mark, my_mark, mk_s, mk_r, k, p) for k, p in enumerate(pix_peers)]

    for load in loads[:3]:
        load.wait()
    for g in gathers:
        g.wait_recv()
    rows = rows_a[...]
    for i, w in enumerate((wq, wk, wv)):
        qkv[:, i * hq : (i + 1) * hq] = jnp.dot(
            rows, w[...], preferred_element_type=F32
        ).astype(BF)

    in_slot = rows_of(qkv_in, t, tile)
    qkv_sends = [
        send(rows_of(qkv, p[1], tile), in_slot, qk_s, qk_r, k, p)
        for k, p in enumerate(pix_peers)
    ]
    in_slot[...] = rows_of(qkv, t, tile)[...]
    for m in mark_sends:
        m.wait_recv()
    lane0 = (lax.broadcasted_iota(jnp.int32, (np_ * tile, 128), 1) == 0).astype(F32).astype(BF)
    alive = (
        lax.dot_general(
            lane0, marks[...], (((1,), (1,)), ((), ())), preferred_element_type=F32
        )
        > 0.5
    )
    for s in qkv_sends:
        s.wait_recv()

    for h in range(heads):
        q = qkv_in[:, h * HD : (h + 1) * HD]
        k = qkv_in[:, hq + h * HD : hq + (h + 1) * HD]
        v = qkv_in[:, 2 * hq + h * HD : 2 * hq + (h + 1) * HD]
        score = lax.dot_general(
            q, k, (((1,), (1,)), ((), ())), preferred_element_type=F32
        ) * HD ** (-0.5)
        masked = jnp.where(alive, score, -1e30)
        top = jnp.max(masked, axis=-1, keepdims=True)
        expo = jnp.where(alive, jnp.exp(masked - top), 0.0)
        total = jnp.sum(expo, axis=-1, keepdims=True)
        mixed = jnp.dot(expo.astype(BF), v, preferred_element_type=F32)
        ctx[:, h * HD : (h + 1) * HD] = (mixed / total).astype(BF)

    ctx_slot = rows_of(ctx_in, t, tile)
    ctx_sends = [
        send(rows_of(ctx, p[1], tile), ctx_slot, cx_s, cx_r, k, p)
        for k, p in enumerate(pix_peers)
    ]
    ctx_slot[...] = rows_of(ctx, t, tile)[...]
    loads[3].wait()
    for s in ctx_sends:
        s.wait_recv()

    def scatter_sum(part, part_in, s_sem, r_sem):
        slot = rows_of(part_in, b, mine)
        sends = [
            send(rows_of(part, p[0], mine), slot, s_sem, r_sem, k, p)
            for k, p in enumerate(band_peers)
        ]
        total = rows_of(part, b, mine)[...].astype(F32)
        for k, s in enumerate(sends):
            s.wait_recv()
            source = lax.rem(b + nb - 1 - k, nb)
            total = total + rows_of(part_in, source, mine)[...].astype(F32)
        return total, sends

    part1[...] = jnp.dot(ctx_in[...], wo[...], preferred_element_type=F32).astype(BF)
    attn_out, sends1 = scatter_sum(part1, part1_in, p1_s, p1_r)
    state = (x_ref[...].astype(F32) + attn_out).astype(BF)

    my_b = rows_of(rows_b, b, mine)
    my_b[...] = normed(state.astype(F32), mgain_ref[...])
    gathers2 = [send(my_b, my_b, bg_s, bg_r, k, p) for k, p in enumerate(band_peers)]
    for load in loads[4:]:
        load.wait()
    for g in gathers2:
        g.wait_recv()
    rows = rows_b[...]
    gate = jnp.dot(rows, wg[...], preferred_element_type=F32)
    upper = jnp.dot(rows, wu[...], preferred_element_type=F32)
    hidden = (gate / (1.0 + jnp.exp(-gate)) * upper).astype(BF)
    part2[...] = jnp.dot(hidden, wd[...], preferred_element_type=F32).astype(BF)
    mlp_out, sends2 = scatter_sum(part2, part2_in, p2_s, p2_r)
    encoded = (state.astype(F32) + mlp_out).astype(BF)
    keep = jnp.concatenate([live[:, :1]] * spec_here, axis=0) > 0
    out_ref[...] = jnp.where(keep, encoded.astype(F32), x_ref[...].astype(F32)).astype(BF)
    for s in gathers + mark_sends + qkv_sends + ctx_sends + sends1 + gathers2 + sends2:
        s.wait_send()


def shards(nb, np_, pixels, clear_count, clear_index, attn_gain, w_query, w_key, w_value, w_out, mlp_gain, w_gate, w_up, w_down):
    tile, spec_here, width = pixels.shape
    spec = spec_here * nb
    mine, rows, slots = spec_here * tile, spec * tile, np_ * tile
    hq = w_query.shape[1]
    weights = (w_query, w_key, w_value, w_out, w_gate, w_up, w_down)
    x = jnp.swapaxes(pixels, 0, 1).reshape(mine, width)
    vmem = pl.BlockSpec(memory_space=pltpu.VMEM)
    smem = pl.BlockSpec(memory_space=pltpu.SMEM)
    dma = pltpu.SemaphoreType.DMA
    out = pl.pallas_call(
        functools.partial(kernel, nb, np_, spec_here, tile, clear_index.shape[0]),
        out_shape=jax.ShapeDtypeStruct((mine, width), BF),
        in_specs=[vmem, smem, smem, vmem, vmem] + [pl.BlockSpec(memory_space=pl.ANY)] * 7,
        out_specs=vmem,
        scratch_shapes=[pltpu.VMEM(w.shape, BF) for w in weights]
        + [
            pltpu.VMEM((rows, width), BF),
            pltpu.VMEM((slots, 128), BF),
            pltpu.VMEM((rows, 3 * hq), BF),
            pltpu.VMEM((slots, 3 * hq), BF),
            pltpu.VMEM((slots, hq), BF),
            pltpu.VMEM((rows, hq), BF),
            pltpu.VMEM((rows, width), BF),
            pltpu.VMEM((rows, width), BF),
            pltpu.VMEM((rows, width), BF),
            pltpu.VMEM((rows, width), BF),
            pltpu.VMEM((rows, width), BF),
            dma((7,)),
        ]
        + [dma((n - 1,)) for n in (nb, np_, np_, np_, nb, nb, nb) for _ in range(2)],
        compiler_params=pltpu.CompilerParams(
            collective_id=0, has_side_effects=True, vmem_limit_bytes=56 * 2**20
        ),
    )(x, clear_count, clear_index, attn_gain.reshape(1, width), mlp_gain.reshape(1, width), *weights)
    return jnp.swapaxes(out.reshape(spec_here, tile, width), 0, 1)


def solution(mesh):
    nb, np_ = mesh.shape["band"], mesh.shape["pix"]
    return jax.shard_map(
        functools.partial(shards, nb, np_),
        mesh=mesh,
        in_specs=(
            P("pix", "band", None),
            P("pix"),
            P("pix"),
            P(),
            P(None, "band"),
            P(None, "band"),
            P(None, "band"),
            P("band", None),
            P(),
            P(None, "band"),
            P(None, "band"),
            P("band", None),
        ),
        out_specs=P("pix", "band", None),
        check_vma=False,
    )
```

time: 140 us -> 42.6 us (0.30)
  blocking collectives: 59.5 us -> 0 us
  waiting for transfers between devices: 45.9 us -> 0 us
  Pallas kernels: 0 us -> 38.7 us
  between operations: 14.3 us -> 0.66 us
  matrix products: 9.32 us -> 0 us
  other arithmetic: 5 us -> 0 us
  local copies, waits for them, and re-layouts: 5.06 us -> 3.02 us
    all_gather x4 -> x0, blocking collectives: 50.8 us -> none  [the longest x1 15.8 us: shards(): key_piece = lax.all_gather(key, 'pix', axis=1, tiled=True)]
    reduce_scatter x2 -> x0, waiting for transfers between devices: 45.8 us -> none  [shards(): lax.psum_scatter(out.reshape(spec_here * lax.axis_size('band'), slots_her...]
    pallas_call x0 -> x1, Pallas kernels: none -> 38.7 us  [shards(): pl.pallas_call(functools.partial(kernel, nb, np_, spec_here, tile, clear_...]
    dot_general x9 -> x0, matrix products: 9.32 us -> none  [the longest x1 3.16 us: shards(): out = jnp.dot(hidden, w_down, preferred_element_type=jnp.float32)]
    unnamed x1 -> x0, blocking collectives: 8.71 us -> none
    convert_element_type x2 -> x0, other arithmetic: 1.77 us -> none  [normed(): return (scaled * gain).astype(jnp.bfloat16)]
    unnamed x19 -> x0, local copies, waits for them, and re-layouts: 1.5 us -> none
    reduce_sum x4 -> x0, other arithmetic: 1.5 us -> none  [the longest x2 1.13 us: normed(): jnp.mean(full * full, axis=-1, keepdims=True) + 1e-05]
  transfers between devices with their start and end apart: 2 -> 0, of which waited for: 2 -> 0; matrix products, arithmetic and copies ran while one was open for 0% -> 0% of each run, Pallas kernels for 0% -> 0%
where the time goes in v1:
time: 42.6 us; the launch traced here: 42.4 us
  Pallas kernels  38.7 us (91%)
  local copies, waits for them, and re-layouts  3.02 us (7%)
  between operations  0.66 us (2%)
    pallas_call x1, Pallas kernels, shards(): pl.pallas_call(functools.partial(kernel, nb, np_, spec_here, tile, clear_...  38.7 us
    reshape x1, local copies, waits for them, and re-layouts, shards(): return jnp.swapaxes(out.reshape(spec_here, tile, width), 0, 1)  1.54 us
    transpose x1, local copies, waits for them, and re-layouts, shards(): x = jnp.swapaxes(pixels, 0, 1).reshape(mine, width)  1.48 us

profile of v1, /device:TPU:0, one launch (start us, length us, event | category | flops | bytes accessed | tf_op | source)
XLA Modules:
  0.0 42.4 jit_solution(15143641131281272709)
XLA Ops:
  0.7 1.5 %copy.13 = bf16[2,16,1024]{2,1,0:T(8,128)(2,1)} copy(bf16[2,16,1024]{2,0,1:T(2,128)(2,1)} %bitcast.10) | data formatting | bytes 131072 | tf_op jit(solution)/shard_map/transpose | solution.py:172
  2.1 38.7 %shard_map.118 = bf16[32,1024]{1,0:T(8,128)(2,1)} custom-call(bf16[32,1024]{1,0:T(8,128)(2,1)} %bitcast.9, s32[1]{0:T(128)S(6)} %copy.17.count_ref, s32[10]{0:T(128)} %index_ref.1, f32[1,1024]{1,0:T(1,128)} %bitcast.11, f32[1,1024]{1,0:T(1,128)} %bitcast.12, bf16[1024,256]{1,0:T(8,128)(2,1)} %wq_h.1, bf16[1024,256]{1,0:T(8,128)(2,1)} %wk_h.1, ...), custom_call_target="tpu_custom_call" | custom-call | tf_op jit(solution)/shard_map/pallas_call | solution.py:176
  40.8 1.5 %copy.16 = bf16[2,16,1024]{2,0,1:T(2,128)(2,1)} copy(bf16[2,16,1024]{2,1,0:T(8,128)(2,1)} %bitcast.8) | data formatting | bytes 131072 | tf_op jit(solution)/shard_map/reshape | solution.py:201

commit v2 on v1

--- a/solution.py
+++ b/solution.py
@@ -20,20 +20,21 @@
 
 def kernel(
     nb, np_, spec_here, tile, caps,
-    x_ref, count_ref, index_ref, again_ref, mgain_ref,
+    pix_h, count_ref, index_ref, again_ref, mgain_ref,
     wq_h, wk_h, wv_h, wo_h, wg_h, wu_h, wd_h,
     out_ref,
     wq, wk, wv, wo, wg, wu, wd,
-    rows_a, marks, qkv, qkv_in, ctx, ctx_in, part1, part1_in, rows_b, part2, part2_in,
+    pix, x_ref, pix_sem, rows_a, marks, qkv, qkv_in, ctx, ctx_in, part1, part1_in, rows_b, part2, part2_in,
     w_sem,
     ag_s, ag_r, mk_s, mk_r, qk_s, qk_r, cx_s, cx_r, p1_s, p1_r, bg_s, bg_r, p2_s, p2_r,
 ):
     b, t = lax.axis_index("band"), lax.axis_index("pix")
     mine = spec_here * tile
-    width = x_ref.shape[1]
     hq = wq.shape[1]
     heads = hq // HD
 
+    pix_load = pltpu.make_async_copy(pix_h, pix, pix_sem)
+    pix_load.start()
     loads = []
     for i, (src, dst) in enumerate(
         ((wq_h, wq), (wk_h, wk), (wv_h, wv), (wo_h, wo), (wg_h, wg), (wu_h, wu), (wd_h, wd))
@@ -42,17 +43,29 @@
         load.start()
         loads.append(load)
 
-    band_peers = [(lax.rem(b + k, nb), t) for k in range(1, nb)]
-    pix_peers = [(b, lax.rem(t + k, np_)) for k in range(1, np_)]
+    def others(me, n):
+        if n & (n - 1) == 0:
+            return [jnp.bitwise_xor(me, k) for k in range(n - 1, 0, -1)]
+        return [lax.rem(me + k, n) for k in range(1, n)]
+
+    def source(me, n, k, peer):
+        return peer if n & (n - 1) == 0 else lax.rem(me + n - 1 - k, n)
+
+    band_peers = [(p, t) for p in others(b, nb)]
+    pix_peers = [(b, p) for p in others(t, np_)]
     barrier = pltpu.get_barrier_semaphore()
-    for peer in band_peers + pix_peers:
+    for peer in pix_peers + band_peers:
         pl.semaphore_signal(barrier, inc=1, device_id=peer, device_id_type=MESH)
 
     def rows_of(ref, i, n):
         return ref.at[pl.ds(pl.multiple_of(i * n, n), n)]
 
     my_rows = rows_of(rows_a, b, mine)
-    my_rows[...] = normed(x_ref[...].astype(F32), again_ref[...])
+    pix_load.wait()
+    raw = pix[...].astype(F32)
+    for s in range(spec_here):
+        x_ref[s * tile : (s + 1) * tile, :] = raw[:, s, :]
+    my_rows[...] = normed(x_ref[...], again_ref[...])
     spot = lax.broadcasted_iota(jnp.int32, (tile, 128), 0)
     count = count_ref[0]
     live = jnp.zeros((tile, 128), jnp.int32)
@@ -135,13 +148,13 @@
         total = rows_of(part, b, mine)[...].astype(F32)
         for k, s in enumerate(sends):
             s.wait_recv()
-            source = lax.rem(b + nb - 1 - k, nb)
-            total = total + rows_of(part_in, source, mine)[...].astype(F32)
+            sender = source(b, nb, k, band_peers[k][0])
+            total = total + rows_of(part_in, sender, mine)[...].astype(F32)
         return total, sends
 
     part1[...] = jnp.dot(ctx_in[...], wo[...], preferred_element_type=F32).astype(BF)
     attn_out, sends1 = scatter_sum(part1, part1_in, p1_s, p1_r)
-    state = (x_ref[...].astype(F32) + attn_out).astype(BF)
+    state = (x_ref[...] + attn_out).astype(BF)
 
     my_b = rows_of(rows_b, b, mine)
     my_b[...] = normed(state.astype(F32), mgain_ref[...])
@@ -158,7 +171,7 @@
     mlp_out, sends2 = scatter_sum(part2, part2_in, p2_s, p2_r)
     encoded = (state.astype(F32) + mlp_out).astype(BF)
     keep = jnp.concatenate([live[:, :1]] * spec_here, axis=0) > 0
-    out_ref[...] = jnp.where(keep, encoded.astype(F32), x_ref[...].astype(F32)).astype(BF)
+    out_ref[...] = jnp.where(keep, encoded.astype(F32), x_ref[...]).astype(BF)
     for s in gathers + mark_sends + qkv_sends + ctx_sends + sends1 + gathers2 + sends2:
         s.wait_send()
 
@@ -169,17 +182,19 @@
     mine, rows, slots = spec_here * tile, spec * tile, np_ * tile
     hq = w_query.shape[1]
     weights = (w_query, w_key, w_value, w_out, w_gate, w_up, w_down)
-    x = jnp.swapaxes(pixels, 0, 1).reshape(mine, width)
     vmem = pl.BlockSpec(memory_space=pltpu.VMEM)
     smem = pl.BlockSpec(memory_space=pltpu.SMEM)
     dma = pltpu.SemaphoreType.DMA
     out = pl.pallas_call(
         functools.partial(kernel, nb, np_, spec_here, tile, clear_index.shape[0]),
         out_shape=jax.ShapeDtypeStruct((mine, width), BF),
-        in_specs=[vmem, smem, smem, vmem, vmem] + [pl.BlockSpec(memory_space=pl.ANY)] * 7,
+        in_specs=[pl.BlockSpec(memory_space=pl.ANY), smem, smem, vmem, vmem] + [pl.BlockSpec(memory_space=pl.ANY)] * 7,
         out_specs=vmem,
         scratch_shapes=[pltpu.VMEM(w.shape, BF) for w in weights]
         + [
+            pltpu.VMEM(pixels.shape, BF),
+            pltpu.VMEM((mine, width), F32),
+            dma(()),
             pltpu.VMEM((rows, width), BF),
             pltpu.VMEM((slots, 128), BF),
             pltpu.VMEM((rows, 3 * hq), BF),
@@ -197,7 +212,7 @@
         compiler_params=pltpu.CompilerParams(
             collective_id=0, has_side_effects=True, vmem_limit_bytes=56 * 2**20
         ),
-    )(x, clear_count, clear_index, attn_gain.reshape(1, width), mlp_gain.reshape(1, width), *weights)
+    )(pixels, clear_count, clear_index, attn_gain.reshape(1, width), mlp_gain.reshape(1, width), *weights)
     return jnp.swapaxes(out.reshape(spec_here, tile, width), 0, 1)
 
 

time: 42.6 us -> 40.2 us (0.944)
  local copies, waits for them, and re-layouts: 3.02 us -> 1.54 us
  Pallas kernels: 38.7 us -> 37.8 us
    transpose x1 -> x0, local copies, waits for them, and re-layouts: 1.48 us -> none  [shards(): x = jnp.swapaxes(pixels, 0, 1).reshape(mine, width)]
    pallas_call x1, Pallas kernels: 38.7 us -> 37.8 us  [shards(): pl.pallas_call(functools.partial(kernel, nb, np_, spec_here, tile, clear_...]
where the time goes in v2:
time: 40.2 us; the launch traced here: 40 us
  Pallas kernels  37.8 us (94%)
  local copies, waits for them, and re-layouts  1.54 us (4%)
  between operations  0.66 us (2%)
    pallas_call x1, Pallas kernels, shards(): pl.pallas_call(functools.partial(kernel, nb, np_, spec_here, tile, clear_...  37.8 us
    reshape x1, local copies, waits for them, and re-layouts, shards(): return jnp.swapaxes(out.reshape(spec_here, tile, width), 0, 1)  1.54 us

profile of v2, /device:TPU:0, one launch (start us, length us, event | category | flops | bytes accessed | tf_op | source)
XLA Modules:
  0.0 40.0 jit_solution(11061054262555437386)
XLA Ops:
  0.7 37.8 %shard_map.118 = bf16[32,1024]{1,0:T(8,128)(2,1)} custom-call(bf16[16,2,1024]{2,1,0:T(2,128)(2,1)} %pix_h.1, s32[1]{0:T(128)S(6)} %copy.16.count_ref, s32[10]{0:T(128)} %index_ref.1, f32[1,1024]{1,0:T(1,128)} %bitcast.7, f32[1,1024]{1,0:T(1,128)} %bitcast.8, bf16[1024,256]{1,0:T(8,128)(2,1)} %wq_h.1, bf16[1024,256]{1,0:T(8,128)(2,1)} %wk_h.1, ...), custom_call_target="tpu_custom_call" | custom-call | tf_op jit(solution)/shard_map/pallas_call | solution.py:188
  38.5 1.5 %copy.15 = bf16[2,16,1024]{2,0,1:T(2,128)(2,1)} copy(bf16[2,16,1024]{2,1,0:T(8,128)(2,1)} %bitcast.6) | data formatting | bytes 131072 | tf_op jit(solution)/shard_map/reshape | solution.py:216

commit v3 on v2

--- a/solution.py
+++ b/solution.py
@@ -29,7 +29,6 @@
     ag_s, ag_r, mk_s, mk_r, qk_s, qk_r, cx_s, cx_r, p1_s, p1_r, bg_s, bg_r, p2_s, p2_r,
 ):
     b, t = lax.axis_index("band"), lax.axis_index("pix")
-    mine = spec_here * tile
     hq = wq.shape[1]
     heads = hq // HD
 
@@ -60,12 +59,14 @@
     def rows_of(ref, i, n):
         return ref.at[pl.ds(pl.multiple_of(i * n, n), n)]
 
-    my_rows = rows_of(rows_a, b, mine)
+    halves = range(spec_here)
+    span = nb * tile
+    z, core = t // spec_here, lax.rem(t, spec_here)
     pix_load.wait()
     raw = pix[...].astype(F32)
-    for s in range(spec_here):
-        x_ref[s * tile : (s + 1) * tile, :] = raw[:, s, :]
-    my_rows[...] = normed(x_ref[...], again_ref[...])
+    for h in halves:
+        x_ref[h * tile : (h + 1) * tile, :] = raw[:, h, :]
+        rows_of(rows_a, h * nb + b, tile)[...] = normed(raw[:, h, :], again_ref[...])
     spot = lax.broadcasted_iota(jnp.int32, (tile, 128), 0)
     count = count_ref[0]
     live = jnp.zeros((tile, 128), jnp.int32)
@@ -76,33 +77,94 @@
 
     pl.semaphore_wait(barrier, len(band_peers) + len(pix_peers))
 
-    def send(src, dst, s_sem, r_sem, k, peer):
-        copy = pltpu.make_async_remote_copy(
-            src_ref=src, dst_ref=dst, send_sem=s_sem.at[k], recv_sem=r_sem.at[k],
+    def link(src, dst, s_sem, r_sem, peer):
+        return pltpu.make_async_remote_copy(
+            src_ref=src, dst_ref=dst, send_sem=s_sem, recv_sem=r_sem,
             device_id=peer, device_id_type=MESH,
         )
+
+    def send(src, dst, s_sem, r_sem, k, peer):
+        copy = link(src, dst, s_sem.at[k], r_sem.at[k], peer)
         copy.start()
         return copy
 
-    gathers = [send(my_rows, my_rows, ag_s, ag_r, k, p) for k, p in enumerate(band_peers)]
+    def gather_half(ref, h, s_sem, r_sem):
+        block = rows_of(ref, h * nb + b, tile)
+        return [
+            send(block, block, s_sem, r_sem, h * (nb - 1) + k, p)
+            for k, p in enumerate(band_peers)
+        ]
+
+    def scatter_half(part, part_in, h, s_sem, r_sem):
+        slot = rows_of(part_in, h * nb + b, tile)
+        return [
+            send(rows_of(part, h * nb + p[0], tile), slot, s_sem, r_sem, h * (nb - 1) + k, p)
+            for k, p in enumerate(band_peers)
+        ]
+
+    def sum_half(part, part_in, h, sends):
+        total = rows_of(part, h * nb + b, tile)[...].astype(F32)
+        for k, s in enumerate(sends):
+            s.wait_recv()
+            sender = source(b, nb, k, band_peers[k][0])
+            total = total + rows_of(part_in, h * nb + sender, tile)[...].astype(F32)
+        return total
+
+    far = range(nb - 1, -1, -1)
+
+    def partner(i, c):
+        return jnp.bitwise_xor(z, i)
+
+    def unless_own(i, c, act):
+        if i == 0:
+            pl.when(core != c)(act)
+        else:
+            act()
+
+    def pix_copies(src, dst_of, s_sem, r_sem, c):
+        made = []
+        for i in far:
+            to = partner(i, c)
+            copy = link(
+                src(to, c), dst_of, s_sem.at[c * nb + i], r_sem.at[core * nb + i],
+                (b, to * spec_here + c),
+            )
+            unless_own(i, c, copy.start)
+            made.append((i, c, copy))
+
+        @pl.when(core == c)
+        def _():
+            dst_of[...] = src(z, c)[...]
+
+        return made
+
+    def pix_wait(ref, s_sem, r_sem, c):
+        block = rows_of(ref, 0, tile)
+        for i in far:
+            copy = link(
+                block, block, s_sem.at[c * nb + i], r_sem.at[c * nb + i],
+                (b, partner(i, c) * spec_here + c),
+            )
+            unless_own(i, c, copy.wait_recv)
+
+    sent = []
+    pix_sent = []
+    gathers = [gather_half(rows_a, h, ag_s, ag_r) for h in halves]
     mark_sends = [send(my_mark, my_mark, mk_s, mk_r, k, p) for k, p in enumerate(pix_peers)]
-
     for load in loads[:3]:
         load.wait()
-    for g in gathers:
-        g.wait_recv()
-    rows = rows_a[...]
-    for i, w in enumerate((wq, wk, wv)):
-        qkv[:, i * hq : (i + 1) * hq] = jnp.dot(
-            rows, w[...], preferred_element_type=F32
-        ).astype(BF)
-
-    in_slot = rows_of(qkv_in, t, tile)
-    qkv_sends = [
-        send(rows_of(qkv, p[1], tile), in_slot, qk_s, qk_r, k, p)
-        for k, p in enumerate(pix_peers)
-    ]
-    in_slot[...] = rows_of(qkv, t, tile)[...]
+    for h in halves:
+        for g in gathers[h]:
+            g.wait_recv()
+        rows = rows_a[h * span : (h + 1) * span, :]
+        for i, w in enumerate((wq, wk, wv)):
+            qkv[h * span : (h + 1) * span, i * hq : (i + 1) * hq] = jnp.dot(
+                rows, w[...], preferred_element_type=F32
+            ).astype(BF)
+        pix_sent += pix_copies(
+            lambda to, c: rows_of(qkv, c * nb + to, tile),
+            rows_of(qkv_in, t, tile), qk_s, qk_r, h,
+        )
     for m in mark_sends:
         m.wait_recv()
     lane0 = (lax.broadcasted_iota(jnp.int32, (np_ * tile, 128), 1) == 0).astype(F32).astype(BF)
@@ -112,8 +174,8 @@
         )
         > 0.5
     )
-    for s in qkv_sends:
-        s.wait_recv()
+    for c in halves:
+        pix_wait(qkv_in, qk_s, qk_r, c)
 
     for h in range(heads):
         q = qkv_in[:, h * HD : (h + 1) * HD]
@@ -129,56 +191,59 @@
         mixed = jnp.dot(expo.astype(BF), v, preferred_element_type=F32)
         ctx[:, h * HD : (h + 1) * HD] = (mixed / total).astype(BF)
 
-    ctx_slot = rows_of(ctx_in, t, tile)
-    ctx_sends = [
-        send(rows_of(ctx, p[1], tile), ctx_slot, cx_s, cx_r, k, p)
-        for k, p in enumerate(pix_peers)
-    ]
-    ctx_slot[...] = rows_of(ctx, t, tile)[...]
+    for c in halves:
+        pix_sent += pix_copies(
+            lambda to, c: rows_of(ctx, to * spec_here + c, tile),
+            rows_of(ctx_in, core * nb + z, tile), cx_s, cx_r, c,
+        )
     loads[3].wait()
-    for s in ctx_sends:
-        s.wait_recv()
-
-    def scatter_sum(part, part_in, s_sem, r_sem):
-        slot = rows_of(part_in, b, mine)
-        sends = [
-            send(rows_of(part, p[0], mine), slot, s_sem, r_sem, k, p)
-            for k, p in enumerate(band_peers)
-        ]
-        total = rows_of(part, b, mine)[...].astype(F32)
-        for k, s in enumerate(sends):
-            s.wait_recv()
-            sender = source(b, nb, k, band_peers[k][0])
-            total = total + rows_of(part_in, sender, mine)[...].astype(F32)
-        return total, sends
-
-    part1[...] = jnp.dot(ctx_in[...], wo[...], preferred_element_type=F32).astype(BF)
-    attn_out, sends1 = scatter_sum(part1, part1_in, p1_s, p1_r)
-    state = (x_ref[...] + attn_out).astype(BF)
-
-    my_b = rows_of(rows_b, b, mine)
-    my_b[...] = normed(state.astype(F32), mgain_ref[...])
-    gathers2 = [send(my_b, my_b, bg_s, bg_r, k, p) for k, p in enumerate(band_peers)]
+    sums = []
+    for h in halves:
+        pix_wait(ctx_in, cx_s, cx_r, h)
+        part1[h * span : (h + 1) * span, :] = jnp.dot(
+            ctx_in[h * span : (h + 1) * span, :], wo[...], preferred_element_type=F32
+        ).astype(BF)
+        sums.append(scatter_half(part1, part1_in, h, p1_s, p1_r))
+    sent += sums
+    states, gathers2 = [], []
+    for h in halves:
+        attn_out = sum_half(part1, part1_in, h, sums[h])
+        state = (x_ref[h * tile : (h + 1) * tile, :] + attn_out).astype(BF).astype(F32)
+        states.append(state)
+        rows_of(rows_b, h * nb + b, tile)[...] = normed(state, mgain_ref[...])
+        gathers2.append(gather_half(rows_b, h, bg_s, bg_r))
     for load in loads[4:]:
         load.wait()
-    for g in gathers2:
-        g.wait_recv()
-    rows = rows_b[...]
-    gate = jnp.dot(rows, wg[...], preferred_element_type=F32)
-    upper = jnp.dot(rows, wu[...], preferred_element_type=F32)
-    hidden = (gate / (1.0 + jnp.exp(-gate)) * upper).astype(BF)
-    part2[...] = jnp.dot(hidden, wd[...], preferred_element_type=F32).astype(BF)
-    mlp_out, sends2 = scatter_sum(part2, part2_in, p2_s, p2_r)
-    encoded = (state.astype(F32) + mlp_out).astype(BF)
-    keep = jnp.concatenate([live[:, :1]] * spec_here, axis=0) > 0
-    out_ref[...] = jnp.where(keep, encoded.astype(F32), x_ref[...]).astype(BF)
-    for s in gathers + mark_sends + qkv_sends + ctx_sends + sends1 + gathers2 + sends2:
-        s.wait_send()
+    sums2 = []
+    for h in halves:
+        for g in gathers2[h]:
+            g.wait_recv()
+        rows = rows_b[h * span : (h + 1) * span, :]
+        gate = jnp.dot(rows, wg[...], preferred_element_type=F32)
+        upper = jnp.dot(rows, wu[...], preferred_element_type=F32)
+        hidden = (gate / (1.0 + jnp.exp(-gate)) * upper).astype(BF)
+        part2[h * span : (h + 1) * span, :] = jnp.dot(
+            hidden, wd[...], preferred_element_type=F32
+        ).astype(BF)
+        sums2.append(scatter_half(part2, part2_in, h, p2_s, p2_r))
+    for h in halves:
+        encoded = (states[h] + sum_half(part2, part2_in, h, sums2[h])).astype(BF)
+        own = slice(h * tile, (h + 1) * tile)
+        out_ref[own, :] = jnp.where(
+            live[:, :1] > 0, encoded.astype(F32), x_ref[own, :]
+        ).astype(BF)
+    for group in gathers + [mark_sends] + sent + gathers2 + sums2:
+        for s in group:
+            s.wait_send()
+    for i, c, copy in pix_sent:
+        unless_own(i, c, copy.wait_send)
 
 
 def shards(nb, np_, pixels, clear_count, clear_index, attn_gain, w_query, w_key, w_value, w_out, mlp_gain, w_gate, w_up, w_down):
     tile, spec_here, width = pixels.shape
     spec = spec_here * nb
+    pairs = spec_here * (nb - 1)
+    assert spec == np_ and nb & (nb - 1) == 0
     mine, rows, slots = spec_here * tile, spec * tile, np_ * tile
     hq = w_query.shape[1]
     weights = (w_query, w_key, w_value, w_out, w_gate, w_up, w_down)
@@ -208,7 +273,7 @@
             pltpu.VMEM((rows, width), BF),
             dma((7,)),
         ]
-        + [dma((n - 1,)) for n in (nb, np_, np_, np_, nb, nb, nb) for _ in range(2)],
+        + [dma((n,)) for n in (pairs, np_ - 1, np_, np_, pairs, pairs, pairs) for _ in range(2)],
         compiler_params=pltpu.CompilerParams(
             collective_id=0, has_side_effects=True, vmem_limit_bytes=56 * 2**20
         ),

time: 40.2 us -> 38.4 us (0.955)
  Pallas kernels: 37.8 us -> 36 us
    pallas_call x1, Pallas kernels: 37.8 us -> 36 us  [shards(): pl.pallas_call(functools.partial(kernel, nb, np_, spec_here, tile, clear_...]
where the time goes in v3:
time: 38.4 us; the launch traced here: 38.2 us
  Pallas kernels  36 us (94%)
  local copies, waits for them, and re-layouts  1.54 us (4%)
  between operations  0.66 us (2%)
    pallas_call x1, Pallas kernels, shards(): pl.pallas_call(functools.partial(kernel, nb, np_, spec_here, tile, clear_...  36 us
    reshape x1, local copies, waits for them, and re-layouts, shards(): return jnp.swapaxes(out.reshape(spec_here, tile, width), 0, 1)  1.54 us

profile of v3, /device:TPU:0, one launch (start us, length us, event | category | flops | bytes accessed | tf_op | source)
XLA Modules:
  0.0 38.2 jit_solution(16960014322269422572)
XLA Ops:
  0.7 36.0 %shard_map.118 = bf16[32,1024]{1,0:T(8,128)(2,1)} custom-call(bf16[16,2,1024]{2,1,0:T(2,128)(2,1)} %pix_h.1, s32[1]{0:T(128)S(6)} %copy.16.count_ref, s32[10]{0:T(128)} %index_ref.1, f32[1,1024]{1,0:T(1,128)} %bitcast.7, f32[1,1024]{1,0:T(1,128)} %bitcast.8, bf16[1024,256]{1,0:T(8,128)(2,1)} %wq_h.1, bf16[1024,256]{1,0:T(8,128)(2,1)} %wk_h.1, ...), custom_call_target="tpu_custom_call" | custom-call | tf_op jit(solution)/shard_map/pallas_call | solution.py:253
  36.7 1.5 %copy.15 = bf16[2,16,1024]{2,0,1:T(2,128)(2,1)} copy(bf16[2,16,1024]{2,1,0:T(8,128)(2,1)} %bitcast.6) | data formatting | bytes 131072 | tf_op jit(solution)/shard_map/reshape | solution.py:281

commit v4 on v3

--- a/solution.py
+++ b/solution.py
@@ -34,6 +34,20 @@
 
     pix_load = pltpu.make_async_copy(pix_h, pix, pix_sem)
     pix_load.start()
+    def others(me, n):
+        if n & (n - 1) == 0:
+            return [jnp.bitwise_xor(me, k) for k in range(n - 1, 0, -1)]
+        return [lax.rem(me + k, n) for k in range(1, n)]
+
+    def source(me, n, k, peer):
+        return peer if n & (n - 1) == 0 else lax.rem(me + n - 1 - k, n)
+
+    band_peers = [(p, t) for p in others(b, nb)]
+    pix_peers = [(b, p) for p in others(t, np_)]
+    barrier = pltpu.get_barrier_semaphore()
+    for peer in pix_peers + band_peers:
+        pl.semaphore_signal(barrier, inc=1, device_id=peer, device_id_type=MESH)
+
     loads = []
     for i, (src, dst) in enumerate(
         ((wq_h, wq), (wk_h, wk), (wv_h, wv), (wo_h, wo), (wg_h, wg), (wu_h, wu), (wd_h, wd))
@@ -41,20 +55,6 @@
         load = pltpu.make_async_copy(src, dst, w_sem.at[i])
         load.start()
         loads.append(load)
-
-    def others(me, n):
-        if n & (n - 1) == 0:
-            return [jnp.bitwise_xor(me, k) for k in range(n - 1, 0, -1)]
-        return [lax.rem(me + k, n) for k in range(1, n)]
-
-    def source(me, n, k, peer):
-        return peer if n & (n - 1) == 0 else lax.rem(me + n - 1 - k, n)
-
-    band_peers = [(p, t) for p in others(b, nb)]
-    pix_peers = [(b, p) for p in others(t, np_)]
-    barrier = pltpu.get_barrier_semaphore()
-    for peer in pix_peers + band_peers:
-        pl.semaphore_signal(barrier, inc=1, device_id=peer, device_id_type=MESH)
 
     def rows_of(ref, i, n):
         return ref.at[pl.ds(pl.multiple_of(i * n, n), n)]

time: 38.4 us -> 38.6 us (level)
  no operation moved by 1% of the time
where the time goes in v4:
time: 38.6 us; the launch traced here: 38.4 us
  Pallas kernels  36.2 us (94%)
  local copies, waits for them, and re-layouts  1.54 us (4%)
  between operations  0.66 us (2%)
    pallas_call x1, Pallas kernels, shards(): pl.pallas_call(functools.partial(kernel, nb, np_, spec_here, tile, clear_...  36.2 us
    reshape x1, local copies, waits for them, and re-layouts, shards(): return jnp.swapaxes(out.reshape(spec_here, tile, width), 0, 1)  1.54 us

profile of v4, /device:TPU:0, one launch (start us, length us, event | category | flops | bytes accessed | tf_op | source)
XLA Modules:
  0.0 38.4 jit_solution(142801109952694989)
XLA Ops:
  0.7 36.2 %shard_map.118 = bf16[32,1024]{1,0:T(8,128)(2,1)} custom-call(bf16[16,2,1024]{2,1,0:T(2,128)(2,1)} %pix_h.1, s32[1]{0:T(128)S(6)} %copy.16.count_ref, s32[10]{0:T(128)} %index_ref.1, f32[1,1024]{1,0:T(1,128)} %bitcast.7, f32[1,1024]{1,0:T(1,128)} %bitcast.8, bf16[1024,256]{1,0:T(8,128)(2,1)} %wq_h.1, bf16[1024,256]{1,0:T(8,128)(2,1)} %wk_h.1, ...), custom_call_target="tpu_custom_call" | custom-call | tf_op jit(solution)/shard_map/pallas_call | solution.py:253
  36.8 1.5 %copy.15 = bf16[2,16,1024]{2,0,1:T(2,128)(2,1)} copy(bf16[2,16,1024]{2,1,0:T(8,128)(2,1)} %bitcast.6) | data formatting | bytes 131072 | tf_op jit(solution)/shard_map/reshape | solution.py:281
